TPU v7x, 32 devices: a whole 2x2x4 slice. The times are simulated.
32 devices in a mesh: dp: 8 (over z, x), tensor: 4 (over y, core).
Axes of the slice: x: 2, y: 2, z: 4, core: 2. Of those that a mesh axis runs over, the one named last changes fastest.
Arguments:
- grads_out: bfloat16 [256, 28672], P('dp'), may hold values from -6 to 6
- inputs: bfloat16 [256, 8192], P('dp'), may hold values from -6 to 6
- basis_out: bfloat16 [28672, 14336], P('dp', 'tensor'), may hold values from -0.03125 to 0.03125
- basis_in: bfloat16 [8192, 4096], P('tensor', 'dp'), may hold values from -0.0625 to 0.0625
- lengths: int32 [8], P('dp'), may hold values from 1 to 32, as said below
Outputs:
- corrections: float32 [14336, 4096], P('tensor', 'dp')
Inputs may be any that keep to these rules, and one draw needn't show every extreme that they name: `lengths`: every sequence has at least one live token, and some sequence has all 32 slots live.
All inputs are finite; a program needn't handle non-finite values.
Results may differ from a plain program's by a relative error of at most 0.0026.
Values may be sent and summed in bfloat16 or wider, within the bound.
A program may use at most 128 MiB of HBM per device.

v0:
```python
import jax
import jax.numpy as jnp
from jax import lax
from jax.sharding import PartitionSpec as P


def per_device(grads_out, inputs, basis_out, basis_in, lengths):
    seq_len = grads_out.shape[0]
    positions = jnp.arange(seq_len)
    live = positions[:, None] < lengths[0]
    masked = jnp.where(live, grads_out, jnp.zeros_like(grads_out))
    gathered = lax.all_to_all(masked, "dp", split_axis=1, concat_axis=0, tiled=True)
    partial_sum = jnp.dot(gathered, basis_out, preferred_element_type=jnp.float32)
    rotated = lax.psum(partial_sum, "dp").astype(jnp.bfloat16)
    width_in = inputs.shape[1] // lax.axis_size("tensor")
    column_slab = lax.dynamic_slice_in_dim(inputs, lax.axis_index("tensor") * width_in, width_in, 1)
    partial_in = jnp.dot(
        lax.all_gather(column_slab, "dp", axis=0, tiled=True),
        basis_in,
        preferred_element_type=jnp.float32,
    )
    panel = lax.psum(partial_in, "tensor").astype(jnp.bfloat16)
    row_total = rotated.shape[0]
    sequences = row_total // seq_len
    group_size = 4
    number_of_blocks = sequences // group_size
    rotated_blocks = rotated.reshape(number_of_blocks, group_size, seq_len, rotated.shape[1])
    panel_block_list = panel.reshape(number_of_blocks, group_size, seq_len, panel.shape[1])

    def accumulate(total, pair):
        left_factor, right_factor = pair
        sample_case = jnp.einsum(
            "qjt,qjr->qtr", left_factor, right_factor, preferred_element_type=jnp.float32
        )
        return (total + jnp.sum(sample_case * sample_case, axis=0), None)

    initial_total = jnp.zeros((rotated.shape[1], panel.shape[1]), jnp.float32)
    total, unused = lax.scan(accumulate, initial_total, (rotated_blocks, panel_block_list))
    return total / row_total


def solution(mesh):
    placed = (P("dp", None), P("dp", None), P("dp", "tensor"), P("tensor", "dp"), P("dp"))
    return jax.shard_map(
        per_device, mesh=mesh, in_specs=placed, out_specs=P("tensor", "dp"), check_vma=False
    )
```

profile of v0, /device:TPU:0, one launch (start us, length us, event | category | flops | bytes accessed | tf_op | source)
XLA Modules:
  0.0 304.5 jit_solution(2250068821605806189)
XLA Ops:
  6.5 0.0 copy-start
  7.4 1.7 broadcast_select_fusion
  9.0 1.4 copy.10
  10.5 7.3 %all-to-all-start = ((bf16[32,8,3584]{2,0,1:T(8,128)(2,1)}), bf16[32,8,3584]{2,0,1:T(8,128)(2,1)}, u32[]{:S(2)}, u32[]{:S(2)}) async-start(bf16[32,8,3584]{2,0,1:T(8,128)(2,1)} %bitcast.25), calls=%async_computation | async-start | bytes 3670016 | tf_op jit(solution)/shard_map/all_to_all | solution.py:12
  17.7 0.0 all-gather.2.cloned.1.call-start
  17.8 1.6 constant_dynamic-slice_fusion
  19.3 0.0 all-gather.2.cloned.1.call-update
  19.4 56.4 %all-gather.2.cloned.1.call-done = bf16[256,2048]{1,0:T(8,128)(2,1)} async-done(((bf16[32,2048]{1,0:T(8,128)(2,1)}), bf16[256,2048]{1,0:T(8,128)(2,1)}) %all-gather.2.cloned.1.call-update) | async-done | bytes 1048592 | tf_op jit(solution)/shard_map/all_gather | solution.py:18
  75.8 0.0 copy-done
  75.8 1.9 fusion.6
  77.7 15.9 %all-reduce.2 = bf16[256,512]{1,0:T(8,128)(2,1)S(1)} all-reduce(f32[256,512]{1,0:T(8,128)S(1)} %fusion.6), channel_id=1, replica_groups=mesh['dp'=8,'tensor'=4] {'tensor'}, use_global_device_ids=true, to_apply=%region_1.2 | all-reduce | flops 131072 | bytes 786432 | tf_op jit(solution)/shard_map/psum | solution.py:22
  93.6 0.0 all-to-all-done
  93.6 13.6 %fusion.5 = f32[256,3584]{1,0:T(8,128)} fusion(bf16[256,3584]{1,0:T(8,128)(2,1)} %bitcast.2, bf16[3584,3584]{1,0:T(8,128)(2,1)} %param.9), kind=kOutput, calls=%fused_computation.12 | convolution fusion | flops 6576668672 | bytes 31195136 | tf_op jit(solution)/shard_map/dot_general | solution.py:13
  107.2 147.5 %all-reduce.3 = bf16[256,3584]{1,0:T(8,128)(2,1)} all-reduce(f32[256,3584]{1,0:T(8,128)} %fusion.5), channel_id=1, replica_groups=mesh['dp'=8,'tensor'=4] {'dp'}, use_global_device_ids=true, to_apply=%region_0.1 | all-reduce | flops 917504 | bytes 5505024 | tf_op jit(solution)/shard_map/psum | solution.py:14
  254.7 35.9 %while.11 = (s32[]{:T(128)}, f32[3584,512]{1,0:T(8,128)}, bf16[2,4,32,3584]{3,2,1,0:T(8,128)(2,1)}, bf16[2,4,32,512]{3,2,1,0:T(8,128)(2,1)S(1)}, s32[]{:T(128)}, /*index=5*/s32[]{:T(128)}) while((s32[]{:T(128)}, f32[3584,512]{1,0:T(8,128)}, bf16[2,4,32,3584]{3,2,1,0:T(8,128)(2,1)}, bf16[2,4,32,512]{3,2,1,0:T(8,128)(2,1)S(1)}, ...), condition=%wide.region_4.5_spmd.clone, body=%wide.region_2.4_spmd.clone.sunk | while | flops 486277120 | bytes 30409812 | solution.py:38
  254.7 8.9 %multiply_reduce_fusion.2 = f32[3584,512]{1,0:T(8,128)} fusion(bf16[2,4,32,3584]{3,2,1,0:T(8,128)(2,1)} %get-tuple-element.90, s32[]{:T(128)S(6)} %copy.15, bf16[2,4,32,512]{3,2,1,0:T(8,128)(2,1)S(1)} %get-tuple-element.91), kind=kOutput, calls=%fused_computation.clone.1 | convolution fusion | flops 482607104 | bytes 8389632 | tf_op jit(solution)/shard_map/while/body/eval_jaxpr/qjt,qjr->qtr/dot_general | solution.py:32
  263.6 8.0 %select_add_fusion.2 = f32[3584,512]{1,0:T(8,128)} fusion(f32[3584,512]{1,0:T(8,128)} %multiply_reduce_fusion.2, f32[3584,512]{1,0:T(8,128)} %get-tuple-element.83, pred[]{:T(512)S(6)} %compare.3), kind=kLoop, calls=%fused_computation.1.clone.1 | loop fusion | flops 3670016 | bytes 22020096 | tf_op jit(solution)/shard_map/while/body/eval_jaxpr/add | solution.py:35
  271.6 8.9 %multiply_reduce_fusion.2 = f32[3584,512]{1,0:T(8,128)} fusion(bf16[2,4,32,3584]{3,2,1,0:T(8,128)(2,1)} %get-tuple-element.90, s32[]{:T(128)S(6)} %copy.15, bf16[2,4,32,512]{3,2,1,0:T(8,128)(2,1)S(1)} %get-tuple-element.91), kind=kOutput, calls=%fused_computation.clone.1 | convolution fusion | flops 482607104 | bytes 8389632 | tf_op jit(solution)/shard_map/while/body/eval_jaxpr/qjt,qjr->qtr/dot_general | solution.py:32
  280.5 10.1 %select_add_fusion.2 = f32[3584,512]{1,0:T(8,128)} fusion(f32[3584,512]{1,0:T(8,128)} %multiply_reduce_fusion.2, f32[3584,512]{1,0:T(8,128)} %get-tuple-element.83, pred[]{:T(512)S(6)} %compare.3), kind=kLoop, calls=%fused_computation.1.clone.1 | loop fusion | flops 3670016 | bytes 22020096 | tf_op jit(solution)/shard_map/while/body/eval_jaxpr/add | solution.py:35
  290.5 7.1 %broadcast_multiply_fusion = f32[3584,512]{1,0:T(8,128)} fusion(f32[3584,512]{1,0:T(8,128)} %get-tuple-element.27), kind=kLoop, calls=%fused_computation.7 | loop fusion | flops 1835008 | bytes 14680064 | tf_op jit(solution)/shard_map/div | solution.py:39
  (2 shorter events, 0.0 us)
Async XLA Ops:
  6.5 69.2 %copy-start = (bf16[2048,512]{1,0:T(8,128)(2,1)S(1)}, bf16[2048,512]{1,0:T(8,128)(2,1)}, u32[]{:S(2)}) copy-start(bf16[2048,512]{1,0:T(8,128)(2,1)} %param.10) | copy-start | bytes 6291460
  10.5 83.2 %all-to-all-start = ((bf16[32,8,3584]{2,0,1:T(8,128)(2,1)}), bf16[32,8,3584]{2,0,1:T(8,128)(2,1)}, u32[]{:S(2)}, u32[]{:S(2)}) async-start(bf16[32,8,3584]{2,0,1:T(8,128)(2,1)} %bitcast.25), calls=%async_computation | async-start | bytes 3670016 | tf_op jit(solution)/shard_map/all_to_all | solution.py:12
  17.7 58.1 %all-gather.2.cloned.1.call-start = ((), (), s32[]{:S(2)}) async-start(), calls=%async_computation.1 | async-start | bytes 1179648 | tf_op jit(solution)/shard_map/all_gather | solution.py:18
Sparse Core Ops, SparseCore 0:
  20.7 55.0 all-gather.1
where the time goes:
time: 305 us; the launch traced here: 304 us
  blocking collectives  163 us (53%)
  waiting for transfers between devices  56.4 us (18%)
  matrix products  33.3 us (11%)
  other arithmetic  26.8 us (9%)
  between operations  14.2 us (5%)
  starting transfers between devices  7.29 us (2%)
    psum x1, blocking collectives, per_device(): rotated = lax.psum(partial_sum, 'dp').astype(jnp.bfloat16)  147 us
    all_gather x1, waiting for transfers between devices, per_device(): lax.all_gather(column_slab, 'dp', axis=0, tiled=True)  56.4 us
    add x2, other arithmetic, accumulate(): return (total + jnp.sum(sample_case * sample_case, axis=0), None)  18.1 us
    dot_general x2, matrix products, accumulate(): jnp.einsum('qjt,qjr->qtr', left_factor, right_factor, preferred_element_t...  17.8 us
    psum x1, blocking collectives, per_device(): panel = lax.psum(partial_in, 'tensor').astype(jnp.bfloat16)  15.9 us
    dot_general x1, matrix products, per_device(): jnp.dot(gathered, basis_out, preferred_element_type=jnp.float32)  13.6 us
    all_to_all x1, starting transfers between devices, per_device(): lax.all_to_all(masked, 'dp', split_axis=1, concat_axis=0, tiled=True)  7.25 us
    div x1, other arithmetic, per_device(): return total / row_total  7.06 us
  transfers between devices with their start and end apart: 2, of which 1 were waited for; matrix products, arithmetic and copies ran while one was open for 1% of the time, Pallas kernels for 0%

commit v1 on v0

v1 whole, which is shorter than its diff:
```python
import functools

import jax
import jax.numpy as jnp
from jax import lax
from jax.experimental import pallas as pl
from jax.experimental.pallas import tpu as pltpu
from jax.sharding import PartitionSpec as P

MESH = pl.DeviceIdType.MESH
BF16 = jnp.bfloat16
F32 = jnp.float32


def ring_to_dp(q, n):
    return jnp.where(q < n // 2, 2 * q, 2 * (n - 1 - q) + 1)


def exchange_kernel(
    n, tn, nc, share_y,
    grads, inputs, basis_out, basis_in, lengths,
    rotated_out, panel_out,
    gathered, basis, slab, basis_small, partial, early_send, early_recv, late_send, late_recv, rotated,
    panel_part, panel_recv, panel,
    a_send, a_recv, fy_send, fy_recv, fc_send, fc_recv, fd_send, fd_recv,
    in_send, in_recv, rs_ssem, rs_rsem, ag_ssem, ag_rsem,
    pr_send, pr_recv, pg_send, pg_recv, local_sem,
):
    d = lax.axis_index("dp")
    t = lax.axis_index("tensor")
    half = n // 2
    length = grads.shape[0]
    hl = length // 2
    width = gathered.shape[1]
    chunk = partial.shape[1] // nc
    slab_width = slab.shape[1]
    z, x = d // 2, d % 2
    pos = jnp.where(x == 0, z, n - 1 - z)
    core = t % 2
    up = t // 2

    def at_ring(offset):
        return ring_to_dp(lax.rem(pos + offset + 2 * n, n), n)

    def rows_of(index, extra=0, size=length):
        return pl.ds(pl.multiple_of(index * length + extra, hl), size)

    basis_copies = []
    pieces = 4
    step_rows = width // pieces
    for i in range(pieces):
        r = pl.ds(i * step_rows, step_rows)
        basis_copies.append(pltpu.make_async_copy(basis_out.at[r], basis.at[r], local_sem.at[i]))
    own_cols = pl.ds(pl.multiple_of(d * width, 128), width)
    own_grads = pltpu.make_async_copy(grads.at[:, own_cols], gathered.at[rows_of(d)], local_sem.at[pieces])
    slab_cols = pl.ds(pl.multiple_of(t * slab_width, 128), slab_width)
    own_slab = pltpu.make_async_copy(inputs.at[:, slab_cols], slab.at[rows_of(d)], local_sem.at[pieces + 1])
    own_small = pltpu.make_async_copy(basis_in, basis_small, local_sem.at[pieces + 2])
    own_grads.start()
    own_slab.start()
    for c in basis_copies:
        c.start()
    own_small.start()

    barrier = pltpu.get_barrier_semaphore()
    for k in range(1, n):
        pl.semaphore_signal(barrier, inc=1, device_id=(lax.rem(d + k, n), t), device_id_type=MESH)
    for k in range(1, tn):
        pl.semaphore_signal(barrier, inc=1, device_id=(d, lax.rem(t + k, tn)), device_id_type=MESH)
    pl.semaphore_wait(barrier, n - 1 + tn - 1)

    piece = width // share_y
    my_y = up if share_y == 2 else 0
    row_extra = core * hl
    mine = pl.ds(pl.multiple_of(my_y * piece, 128), piece)
    other = pl.ds(pl.multiple_of((1 - my_y) * piece, 128), piece)

    def a_copy(k, source, target):
        cols = pl.ds(pl.multiple_of(target * width + my_y * piece, 128), piece)
        return pltpu.make_async_remote_copy(
            src_ref=grads.at[pl.ds(pl.multiple_of(row_extra, hl), hl), cols],
            dst_ref=gathered.at[rows_of(source, row_extra, hl), mine],
            send_sem=a_send.at[k], recv_sem=a_recv.at[k],
            device_id=(target, t), device_id_type=MESH)

    def forward(k, extra, cols, ssem, rsem, target_t):
        ref = gathered.at[rows_of(lax.rem(d - k + n, n), extra, hl), cols]
        return pltpu.make_async_remote_copy(
            src_ref=ref, dst_ref=ref, send_sem=ssem.at[k], recv_sem=rsem.at[k],
            device_id=(d, target_t), device_id_type=MESH)

    partner = up * 2 + (1 - core)
    across = lax.rem(t + 2, tn)
    order = []
    for k in range(1, n // 2 + 1):
        order.append(k)
        if n - k != k:
            order.append(n - k)
    order = order[::-1]
    for k in order:
        a_copy(k, d, lax.rem(d + k, n)).start()

    def in_copy(direction, s, receiving):
        sign = 1 if direction == 0 else -1
        q = (-sign) * (s + 1 if receiving else s)
        last = s == half - 1
        extra = direction * hl if last else 0
        ref = slab.at[rows_of(at_ring(q), extra, hl if last else length)]
        return pltpu.make_async_remote_copy(
            src_ref=ref, dst_ref=ref, send_sem=in_send.at[direction, s], recv_sem=in_recv.at[direction, s],
            device_id=(at_ring(sign), t), device_id_type=MESH)

    own_slab.wait()
    for direction in range(2):
        in_copy(direction, 0, False).start()

    for k in order:
        a_copy(k, lax.rem(d - k + n, n), d).wait_recv()
        if share_y == 2:
            forward(k, row_extra, mine, fy_send, fy_recv, across).start()
        forward(k, row_extra, mine, fc_send, fc_recv, partner).start()
    if share_y == 2:
        for k in order:
            forward(k, row_extra, other, fy_send, fy_recv, across).wait_recv()
            forward(k, row_extra, other, fd_send, fd_recv, partner).start()
    there = hl - row_extra
    for k in order:
        forward(k, there, mine, fc_send, fc_recv, partner).wait_recv()
        if share_y == 2:
            forward(k, there, other, fd_send, fd_recv, partner).wait_recv()
    own_grads.wait()
    for c in basis_copies:
        c.wait()

    early = early_send.shape[1]

    def rs_send(direction, s, c):
        return early_send.at[direction, s, c] if s < early else late_send.at[direction, s - early, c]

    def rs_recv(direction, s, c):
        return early_recv.at[direction, s, c] if s < early else late_recv.at[direction, s - early, c]

    def rs_copy(direction, s, c):
        size = hl if s == 0 else length
        r = pl.ds(0, size)
        sign = 1 if direction == 0 else -1
        return pltpu.make_async_remote_copy(
            src_ref=rs_send(direction, s, c).at[r], dst_ref=rs_recv(direction, s, c).at[r],
            send_sem=rs_ssem.at[direction, s, c], recv_sem=rs_rsem.at[direction, s, c],
            device_id=(at_ring(sign), t), device_id_type=MESH)

    def cols_of(c):
        return pl.ds(pl.multiple_of(c * chunk, 128), chunk)

    def rotate(c):
        cols = cols_of(c)
        partial[:, cols] = jnp.dot(gathered[...], basis[:, cols], preferred_element_type=F32)
        target = at_ring(half)
        for direction in range(2):
            early_send[direction, 0, c, :hl] = partial[rows_of(target, direction * hl, hl), cols].astype(BF16)
            rs_copy(direction, 0, c).start()

    done = 0
    for s in range(1, half):
        until = max(done, min(nc, (2 * s) if nc > 2 else 1))
        if until > done:
            lax.fori_loop(done, until, lambda c, u: (rotate(c), u)[1], 0)
        done = until
        for direction in range(2):
            in_copy(direction, s - 1, True).wait_recv()
            in_copy(direction, s, False).start()
    if done < nc:
        lax.fori_loop(done, nc, lambda c, u: (rotate(c), u)[1], 0)

    for direction in range(2):
        in_copy(direction, half - 1, True).wait_recv()
    own_small.wait()
    panel_part[...] = jnp.dot(slab[...], basis_small[...], preferred_element_type=F32)
    share = panel_part.shape[0] // tn

    def share_rows(index):
        return pl.ds(pl.multiple_of(index * share, 16), share)

    def pr_copy(k):
        target = lax.rem(t + k, tn)
        return pltpu.make_async_remote_copy(
            src_ref=panel_part.at[share_rows(target)], dst_ref=panel_recv.at[k],
            send_sem=pr_send.at[k], recv_sem=pr_recv.at[k],
            device_id=(d, target), device_id_type=MESH)

    def pg_copy(k, source):
        ref = panel.at[share_rows(source)]
        return pltpu.make_async_remote_copy(
            src_ref=ref, dst_ref=ref, send_sem=pg_send.at[k], recv_sem=pg_recv.at[k],
            device_id=(d, lax.rem(t + k, tn)), device_id_type=MESH)

    for k in range(1, tn):
        pr_copy(k).start()

    for s in range(1, half):
        def reduce_step(c, u, s=s):
            cols = cols_of(c)
            for direction in range(2):
                sign = 1 if direction == 0 else -1
                target = at_ring(sign * (half - s))
                rs_copy(direction, s - 1, c).wait_recv()
                if s == 1:
                    near = slice(0, hl) if direction == 0 else slice(hl, length)
                    far = slice(hl, length) if direction == 0 else slice(0, hl)
                    near_at, far_at = direction * hl, (1 - direction) * hl
                    early_send[direction, s, c, near] = (
                        partial[rows_of(target, near_at, hl), cols]
                        + early_recv[direction, 0, c, :hl].astype(F32)).astype(BF16)
                    early_send[direction, s, c, far] = partial[rows_of(target, far_at, hl), cols].astype(BF16)
                else:
                    late_send[direction, s - early, c] = (
                        partial[rows_of(target), cols] + rs_recv(direction, s - 1, c)[...].astype(F32))
                rs_copy(direction, s, c).start()
            return u
        lax.fori_loop(0, nc, reduce_step, 0)
        if s == 1:
            total = panel_part[share_rows(t)]
            for k in range(1, tn):
                pr_copy(k).wait_recv()
                total = total + panel_recv[k]
            panel[share_rows(t)] = total.astype(BF16)
            for k in range(1, tn):
                pg_copy(k, t).start()

    def ag_copy(direction, s, c, receiving):
        sign = 1 if direction == 0 else -1
        q = (-sign) * (s + 1 if receiving else s)
        last = s == half - 1
        extra = direction * hl if last else 0
        ref = rotated.at[c, rows_of(at_ring(q), extra, hl if last else length)]
        return pltpu.make_async_remote_copy(
            src_ref=ref, dst_ref=ref, send_sem=ag_ssem.at[direction, s, c], recv_sem=ag_rsem.at[direction, s, c],
            device_id=(at_ring(sign), t), device_id_type=MESH)

    live = lax.broadcasted_iota(jnp.int32, (length, chunk), 0) < lengths[0]

    def finish(c, u):
        cols = cols_of(c)
        for direction in range(2):
            rs_copy(direction, half - 1, c).wait_recv()
        total = partial[rows_of(d), cols]
        total = total + rs_recv(0, half - 1, c)[...] + rs_recv(1, half - 1, c)[...]
        rotated[c, rows_of(d)] = jnp.where(live, total, 0.0).astype(BF16)
        for direction in range(2):
            ag_copy(direction, 0, c, False).start()
        return u
    lax.fori_loop(0, nc, finish, 0)
    for s in range(1, half):
        def pass_on(c, u, s=s):
            for direction in range(2):
                ag_copy(direction, s - 1, c, True).wait_recv()
                ag_copy(direction, s, c, False).start()
            return u
        lax.fori_loop(0, nc, pass_on, 0)

    for k in range(1, tn):
        pg_copy(k, lax.rem(t - k + tn, tn)).wait_recv()
    panel_store = pltpu.make_async_copy(panel, panel_out, local_sem.at[pieces + 3])
    panel_store.start()

    def last_step(c, u):
        for direction in range(2):
            ag_copy(direction, half - 1, c, True).wait_recv()
        return u
    lax.fori_loop(0, nc, last_step, 0)
    rotated_store = pltpu.make_async_copy(rotated, rotated_out, local_sem.at[pieces + 4])
    rotated_store.start()

    for k in order:
        a_copy(k, d, lax.rem(d + k, n)).wait_send()
        forward(k, row_extra, mine, fc_send, fc_recv, partner).wait_send()
        if share_y == 2:
            forward(k, row_extra, mine, fy_send, fy_recv, across).wait_send()
            forward(k, row_extra, other, fd_send, fd_recv, partner).wait_send()
    for s in range(half):
        for direction in range(2):
            in_copy(direction, s, False).wait_send()

        def sent(c, u, s=s):
            for direction in range(2):
                rs_copy(direction, s, c).wait_send()
                ag_copy(direction, s, c, False).wait_send()
            return u
        lax.fori_loop(0, nc, sent, 0)
    for k in range(1, tn):
        pr_copy(k).wait_send()
        pg_copy(k, t).wait_send()
    panel_store.wait()
    rotated_store.wait()


def square_kernel(sequences, length, scale, rotated, panel, out):
    total = None
    for s in range(sequences):
        r = slice(s * length, (s + 1) * length)
        example = lax.dot_general(
            rotated[0, r, :], panel[r, :], (((0,), (0,)), ((), ())), preferred_element_type=F32)
        total = example * example if total is None else total + example * example
    out[...] = total * scale


def pick_chunk(width):
    for size in (512, 256, 128):
        if width % size == 0:
            return size
    return width


def per_device(grads_out, inputs, basis_out, basis_in, lengths):
    n, tn = lax.axis_size("dp"), lax.axis_size("tensor")
    length = grads_out.shape[0]
    rows = n * length
    width, columns = basis_out.shape
    slab_width, panel_width = basis_in.shape
    half = n // 2
    chunk = pick_chunk(columns) if n <= 8 else columns
    nc = columns // chunk
    share_y = 2 if tn == 4 and width % 256 == 0 else 1
    dma = pltpu.SemaphoreType.DMA
    anywhere = pl.BlockSpec(memory_space=pl.ANY)
    flops = 2 * rows * width * columns + 2 * rows * slab_width * panel_width
    rotated, panel = pl.pallas_call(
        functools.partial(exchange_kernel, n, tn, nc, share_y),
        out_shape=(
            jax.ShapeDtypeStruct((nc, rows, chunk), BF16),
            jax.ShapeDtypeStruct((rows, panel_width), BF16),
        ),
        in_specs=[anywhere] * 4 + [pl.BlockSpec(memory_space=pltpu.SMEM)],
        out_specs=(anywhere, anywhere),
        scratch_shapes=[
            pltpu.VMEM((rows, width), BF16),
            pltpu.VMEM((width, columns), BF16),
            pltpu.VMEM((rows, slab_width), BF16),
            pltpu.VMEM((slab_width, panel_width), BF16),
            pltpu.VMEM((rows, columns), F32),
            pltpu.VMEM((2, 2, nc, length, chunk), BF16),
            pltpu.VMEM((2, 2, nc, length, chunk), BF16),
            pltpu.VMEM((2, half - 2, nc, length, chunk), F32),
            pltpu.VMEM((2, half - 2, nc, length, chunk), F32),
            pltpu.VMEM((nc, rows, chunk), BF16),
            pltpu.VMEM((rows, panel_width), F32),
            pltpu.VMEM((tn, rows // tn, panel_width), F32),
            pltpu.VMEM((rows, panel_width), BF16),
            dma((n,)), dma((n,)), dma((n,)), dma((n,)), dma((n,)), dma((n,)), dma((n,)), dma((n,)),
            dma((2, half)), dma((2, half)),
            dma((2, half, nc)), dma((2, half, nc)), dma((2, half, nc)), dma((2, half, nc)),
            dma((tn,)), dma((tn,)), dma((tn,)), dma((tn,)),
            dma((9,)),
        ],
        cost_estimate=pl.CostEstimate(
            flops=flops, bytes_accessed=2 * (width * columns + slab_width * panel_width), transcendentals=0),
        compiler_params=pltpu.CompilerParams(
            collective_id=0, has_side_effects=True, vmem_limit_bytes=56 * 1024 * 1024),
        name="exchange",
    )(grads_out, inputs, basis_out, basis_in, lengths)
    return pl.pallas_call(
        functools.partial(square_kernel, n, length, 1.0 / rows),
        out_shape=jax.ShapeDtypeStruct((columns, panel_width), F32),
        grid=(nc,),
        in_specs=[
            pl.BlockSpec((1, rows, chunk), lambda i: (i, 0, 0)),
            pl.BlockSpec((rows, panel_width), lambda i: (0, 0)),
        ],
        out_specs=pl.BlockSpec((chunk, panel_width), lambda i: (i, 0)),
        cost_estimate=pl.CostEstimate(
            flops=2 * rows * columns * panel_width, bytes_accessed=4 * columns * panel_width, transcendentals=0),
        compiler_params=pltpu.CompilerParams(vmem_limit_bytes=48 * 1024 * 1024),
        name="square_sum",
    )(rotated, panel)


def solution(mesh):
    placed = (P("dp", None), P("dp", None), P("dp", "tensor"), P("tensor", "dp"), P("dp"))
    return jax.shard_map(
        per_device, mesh=mesh, in_specs=placed, out_specs=P("tensor", "dp"), check_vma=False
    )
```

time: 305 us -> 103 us (0.34)
  blocking collectives: 163 us -> 0 us
  Pallas kernels: 0 us -> 99.1 us
  waiting for transfers between devices: 56.4 us -> 0 us
  matrix products: 33.3 us -> 0 us
  other arithmetic: 26.8 us -> 0 us
  between operations: 14.2 us -> 0.67 us
  starting transfers between devices: 7.29 us -> 0 us
    psum x2 -> x0, blocking collectives: 163 us -> none  [the longest x1 147 us: per_device(): rotated = lax.psum(partial_sum, 'dp').astype(jnp.bfloat16)]
    pallas_call x0 -> x2, Pallas kernels: none -> 99.1 us  [the longest x1 89.1 us: per_device(): pl.pallas_call(functools.partial(exchange_kernel, n, tn, nc, share_y), ou...]
    all_gather x1 -> x0, waiting for transfers between devices: 56.4 us -> none  [per_device(): lax.all_gather(column_slab, 'dp', axis=0, tiled=True)]
    dot_general x4 -> x0, matrix products: 33.3 us -> none  [the longest x2 17.8 us: accumulate(): jnp.einsum('qjt,qjr->qtr', left_factor, right_factor, preferred_element_t...]
    add x2 -> x0, other arithmetic: 18.1 us -> none  [accumulate(): return (total + jnp.sum(sample_case * sample_case, axis=0), None)]
    all_to_all x1 -> x0, starting transfers between devices: 7.25 us -> none  [per_device(): lax.all_to_all(masked, 'dp', split_axis=1, concat_axis=0, tiled=True)]
    div x1 -> x0, other arithmetic: 7.06 us -> none  [per_device(): return total / row_total]
  transfers between devices with their start and end apart: 2 -> 0, of which waited for: 1 -> 0; matrix products, arithmetic and copies ran while one was open for 1% -> 0% of each run, Pallas kernels for 0% -> 0%
where the time goes in v1:
time: 103 us; the launch traced here: 102 us
  Pallas kernels  99.1 us (96%)
  local copies, waits for them, and re-layouts  2.44 us (2%)
    pallas_call x1, Pallas kernels, per_device(): pl.pallas_call(functools.partial(exchange_kernel, n, tn, nc, share_y), ou...  89.1 us
    pallas_call x1, Pallas kernels, per_device(): pl.pallas_call(functools.partial(square_kernel, n, length, 1.0 / rows), o...  9.98 us
    unnamed x4, local copies, waits for them, and re-layouts  2.44 us

profile of v1, /device:TPU:0, one launch (start us, length us, event | category | flops | bytes accessed | tf_op | source)
XLA Modules:
  0.0 102.2 jit_solution(1717668330782981361)
XLA Ops:
  0.7 89.1 %exchange.1 = (bf16[7,256,512]{2,1,0:T(8,128)(2,1)}, bf16[256,512]{1,0:T(8,128)(2,1)}) custom-call(bf16[32,28672]{1,0:T(8,128)(2,1)} %grads.1, bf16[32,8192]{1,0:T(8,128)(2,1)} %inputs.1, bf16[3584,3584]{1,0:T(8,128)(2,1)} %basis_out.1, bf16[2048,512]{1,0:T(8,128)(2,1)} %basis_in.1, s32[1]{0:T(128)S(6)} %copy.6.lengths), custom_call_target="tpu_custom_call" | custom-call | flops 7113539584 | bytes 27787264 | tf_op jit(solution)/shard_map/exchange/pallas_call | solution.py:327
  89.8 0.0 copy-start
  89.8 1.5 %copy-done = bf16[7,256,512]{2,1,0:T(8,128)(2,1)S(1)} copy-done((bf16[7,256,512]{2,1,0:T(8,128)(2,1)S(1)}, bf16[7,256,512]{2,1,0:T(8,128)(2,1)}, u32[]{:S(2)}) %copy-start) | copy-done | bytes 1835032
  91.3 0.0 copy-start.1
  91.3 0.9 copy-done.1
  92.2 10.0 %square_sum.1 = f32[3584,512]{1,0:T(8,128)} custom-call(bf16[7,256,512]{2,1,0:T(8,128)(2,1)S(1)} %copy-done, bf16[256,512]{1,0:T(8,128)(2,1)S(1)} %copy-done.1), custom_call_target="tpu_custom_call" | custom-call | flops 939524096 | bytes 7340032 | tf_op jit(solution)/shard_map/square_sum/pallas_call | solution.py:361
Async XLA Ops:
  89.8 1.5 %copy-start = (bf16[7,256,512]{2,1,0:T(8,128)(2,1)S(1)}, bf16[7,256,512]{2,1,0:T(8,128)(2,1)}, u32[]{:S(2)}) copy-start(bf16[7,256,512]{2,1,0:T(8,128)(2,1)} %get-tuple-element.7.rotated) | copy-start | bytes 5505028
  91.3 0.9 copy-start.1

commit v2 on v1

--- a/solution.py
+++ b/solution.py
@@ -19,9 +19,9 @@
 def exchange_kernel(
     n, tn, nc, share_y,
     grads, inputs, basis_out, basis_in, lengths,
-    rotated_out, panel_out,
+    summed_out, last_rotated, last_panel,
     gathered, basis, slab, basis_small, partial, early_send, early_recv, late_send, late_recv, rotated,
-    panel_part, panel_recv, panel,
+    panel_part, panel_recv, panel, summed,
     a_send, a_recv, fy_send, fy_recv, fc_send, fc_recv, fd_send, fd_recv,
     in_send, in_recv, rs_ssem, rs_rsem, ag_ssem, ag_rsem,
     pr_send, pr_recv, pg_send, pg_recv, local_sem,
@@ -119,18 +119,33 @@
         if share_y == 2:
             forward(k, row_extra, mine, fy_send, fy_recv, across).start()
         forward(k, row_extra, mine, fc_send, fc_recv, partner).start()
-    if share_y == 2:
-        for k in order:
-            forward(k, row_extra, other, fy_send, fy_recv, across).wait_recv()
-            forward(k, row_extra, other, fd_send, fd_recv, partner).start()
     there = hl - row_extra
     for k in order:
         forward(k, there, mine, fc_send, fc_recv, partner).wait_recv()
-        if share_y == 2:
-            forward(k, there, other, fd_send, fd_recv, partner).wait_recv()
     own_grads.wait()
     for c in basis_copies:
         c.wait()
+
+    def cols_of(c):
+        return pl.ds(pl.multiple_of(c * chunk, 128), chunk)
+
+    if share_y == 2:
+        def pass_across(i):
+            k = jnp.where(i % 2 == 1, half + (i + 1) // 2, half - i // 2)
+            forward(k, row_extra, other, fy_send, fy_recv, across).wait_recv()
+            forward(k, row_extra, other, fd_send, fd_recv, partner).start()
+
+        def first_half(c):
+            cols = cols_of(c)
+            partial[:, cols] = jnp.dot(gathered[:, mine], basis[mine, cols], preferred_element_type=F32)
+
+        if nc == n - 1:
+            lax.fori_loop(0, nc, lambda i, u: (first_half(i), pass_across(i), u)[2], 0)
+        else:
+            lax.fori_loop(0, n - 1, lambda i, u: (pass_across(i), u)[1], 0)
+            lax.fori_loop(0, nc, lambda i, u: (first_half(i), u)[1], 0)
+        for k in order:
+            forward(k, there, other, fd_send, fd_recv, partner).wait_recv()
 
     early = early_send.shape[1]
 
@@ -149,12 +164,12 @@
             send_sem=rs_ssem.at[direction, s, c], recv_sem=rs_rsem.at[direction, s, c],
             device_id=(at_ring(sign), t), device_id_type=MESH)
 
-    def cols_of(c):
-        return pl.ds(pl.multiple_of(c * chunk, 128), chunk)
-
     def rotate(c):
         cols = cols_of(c)
-        partial[:, cols] = jnp.dot(gathered[...], basis[:, cols], preferred_element_type=F32)
+        if share_y == 2:
+            partial[:, cols] += jnp.dot(gathered[:, other], basis[other, cols], preferred_element_type=F32)
+        else:
+            partial[:, cols] = jnp.dot(gathered[...], basis[:, cols], preferred_element_type=F32)
         target = at_ring(half)
         for direction in range(2):
             early_send[direction, 0, c, :hl] = partial[rows_of(target, direction * hl, hl), cols].astype(BF16)
@@ -237,6 +252,15 @@
             src_ref=ref, dst_ref=ref, send_sem=ag_ssem.at[direction, s, c], recv_sem=ag_rsem.at[direction, s, c],
             device_id=(at_ring(sign), t), device_id_type=MESH)
 
+    for k in range(1, tn):
+        pg_copy(k, lax.rem(t - k + tn, tn)).wait_recv()
+
+    def square(c, index):
+        example = lax.dot_general(
+            rotated[c, rows_of(index)], panel[rows_of(index)], (((0,), (0,)), ((), ())),
+            preferred_element_type=F32)
+        return example * example
+
     live = lax.broadcasted_iota(jnp.int32, (length, chunk), 0) < lengths[0]
 
     def finish(c, u):
@@ -248,6 +272,7 @@
         rotated[c, rows_of(d)] = jnp.where(live, total, 0.0).astype(BF16)
         for direction in range(2):
             ag_copy(direction, 0, c, False).start()
+        summed[cols] = square(c, d)
         return u
     lax.fori_loop(0, nc, finish, 0)
     for s in range(1, half):
@@ -255,12 +280,14 @@
             for direction in range(2):
                 ag_copy(direction, s - 1, c, True).wait_recv()
                 ag_copy(direction, s, c, False).start()
+            summed[cols_of(c)] += square(c, at_ring(-s)) + square(c, at_ring(s))
             return u
         lax.fori_loop(0, nc, pass_on, 0)
 
-    for k in range(1, tn):
-        pg_copy(k, lax.rem(t - k + tn, tn)).wait_recv()
-    panel_store = pltpu.make_async_copy(panel, panel_out, local_sem.at[pieces + 3])
+    summed_store = pltpu.make_async_copy(summed, summed_out, local_sem.at[pieces + 3])
+    summed_store.start()
+    last_rows = rows_of(at_ring(half))
+    panel_store = pltpu.make_async_copy(panel.at[last_rows], last_panel, local_sem.at[pieces + 4])
     panel_store.start()
 
     def last_step(c, u):
@@ -268,7 +295,7 @@
             ag_copy(direction, half - 1, c, True).wait_recv()
         return u
     lax.fori_loop(0, nc, last_step, 0)
-    rotated_store = pltpu.make_async_copy(rotated, rotated_out, local_sem.at[pieces + 4])
+    rotated_store = pltpu.make_async_copy(rotated.at[:, last_rows], last_rotated, local_sem.at[pieces + 5])
     rotated_store.start()
 
     for k in order:
@@ -290,18 +317,15 @@
     for k in range(1, tn):
         pr_copy(k).wait_send()
         pg_copy(k, t).wait_send()
+    summed_store.wait()
     panel_store.wait()
     rotated_store.wait()
 
 
-def square_kernel(sequences, length, scale, rotated, panel, out):
-    total = None
-    for s in range(sequences):
-        r = slice(s * length, (s + 1) * length)
-        example = lax.dot_general(
-            rotated[0, r, :], panel[r, :], (((0,), (0,)), ((), ())), preferred_element_type=F32)
-        total = example * example if total is None else total + example * example
-    out[...] = total * scale
+def finish_kernel(scale, summed, rotated, panel, out):
+    example = lax.dot_general(
+        rotated[0], panel[...], (((0,), (0,)), ((), ())), preferred_element_type=F32)
+    out[...] = (summed[...] + example * example) * scale
 
 
 def pick_chunk(width):
@@ -324,14 +348,15 @@
     dma = pltpu.SemaphoreType.DMA
     anywhere = pl.BlockSpec(memory_space=pl.ANY)
     flops = 2 * rows * width * columns + 2 * rows * slab_width * panel_width
-    rotated, panel = pl.pallas_call(
+    summed, last_rotated, last_panel = pl.pallas_call(
         functools.partial(exchange_kernel, n, tn, nc, share_y),
         out_shape=(
-            jax.ShapeDtypeStruct((nc, rows, chunk), BF16),
-            jax.ShapeDtypeStruct((rows, panel_width), BF16),
+            jax.ShapeDtypeStruct((columns, panel_width), F32),
+            jax.ShapeDtypeStruct((nc, length, chunk), BF16),
+            jax.ShapeDtypeStruct((length, panel_width), BF16),
         ),
         in_specs=[anywhere] * 4 + [pl.BlockSpec(memory_space=pltpu.SMEM)],
-        out_specs=(anywhere, anywhere),
+        out_specs=(anywhere, anywhere, anywhere),
         scratch_shapes=[
             pltpu.VMEM((rows, width), BF16),
             pltpu.VMEM((width, columns), BF16),
@@ -346,32 +371,34 @@
             pltpu.VMEM((rows, panel_width), F32),
             pltpu.VMEM((tn, rows // tn, panel_width), F32),
             pltpu.VMEM((rows, panel_width), BF16),
+            pltpu.VMEM((columns, panel_width), F32),
             dma((n,)), dma((n,)), dma((n,)), dma((n,)), dma((n,)), dma((n,)), dma((n,)), dma((n,)),
             dma((2, half)), dma((2, half)),
             dma((2, half, nc)), dma((2, half, nc)), dma((2, half, nc)), dma((2, half, nc)),
             dma((tn,)), dma((tn,)), dma((tn,)), dma((tn,)),
-            dma((9,)),
+            dma((10,)),
         ],
         cost_estimate=pl.CostEstimate(
             flops=flops, bytes_accessed=2 * (width * columns + slab_width * panel_width), transcendentals=0),
         compiler_params=pltpu.CompilerParams(
-            collective_id=0, has_side_effects=True, vmem_limit_bytes=56 * 1024 * 1024),
+            collective_id=0, has_side_effects=True, vmem_limit_bytes=60 * 1024 * 1024),
         name="exchange",
     )(grads_out, inputs, basis_out, basis_in, lengths)
     return pl.pallas_call(
-        functools.partial(square_kernel, n, length, 1.0 / rows),
+        functools.partial(finish_kernel, 1.0 / rows),
         out_shape=jax.ShapeDtypeStruct((columns, panel_width), F32),
         grid=(nc,),
         in_specs=[
-            pl.BlockSpec((1, rows, chunk), lambda i: (i, 0, 0)),
-            pl.BlockSpec((rows, panel_width), lambda i: (0, 0)),
+            pl.BlockSpec((chunk, panel_width), lambda i: (i, 0)),
+            pl.BlockSpec((1, length, chunk), lambda i: (i, 0, 0)),
+            pl.BlockSpec((length, panel_width), lambda i: (0, 0)),
         ],
         out_specs=pl.BlockSpec((chunk, panel_width), lambda i: (i, 0)),
         cost_estimate=pl.CostEstimate(
-            flops=2 * rows * columns * panel_width, bytes_accessed=4 * columns * panel_width, transcendentals=0),
-        compiler_params=pltpu.CompilerParams(vmem_limit_bytes=48 * 1024 * 1024),
-        name="square_sum",
-    )(rotated, panel)
+            flops=2 * length * columns * panel_width, bytes_accessed=8 * columns * panel_width, transcendentals=0),
+        compiler_params=pltpu.CompilerParams(vmem_limit_bytes=60 * 1024 * 1024),
+        name="finish",
+    )(summed, last_rotated, last_panel)
 
 
 def solution(mesh):

time: 103 us -> 99.8 us (0.969)
  local copies, waits for them, and re-layouts: 2.44 us -> 0 us
    unnamed x4 -> x0, local copies, waits for them, and re-layouts: 2.44 us -> none
where the time goes in v2:
time: 99.8 us; the launch traced here: 99.2 us
  Pallas kernels  98.5 us (99%)
    pallas_call x1, Pallas kernels, per_device(): pl.pallas_call(functools.partial(exchange_kernel, n, tn, nc, share_y), ou...  89 us
    pallas_call x1, Pallas kernels, per_device(): pl.pallas_call(functools.partial(finish_kernel, 1.0 / rows), out_shape=ja...  9.53 us

profile of v2, /device:TPU:0, one launch (start us, length us, event | category | flops | bytes accessed | tf_op | source)
XLA Modules:
  0.0 99.2 jit_solution(9798291700374602934)
XLA Ops:
  0.7 89.0 %exchange.1 = (f32[3584,512]{1,0:T(8,128)}, bf16[7,32,512]{2,1,0:T(8,128)(2,1)}, bf16[32,512]{1,0:T(8,128)(2,1)}) custom-call(bf16[32,28672]{1,0:T(8,128)(2,1)} %grads.1, bf16[32,8192]{1,0:T(8,128)(2,1)} %inputs.1, bf16[3584,3584]{1,0:T(8,128)(2,1)} %basis_out.1, bf16[2048,512]{1,0:T(8,128)(2,1)} %basis_in.1, s32[1]{0:T(128)S(6)} %copy.6.lengths), custom_call_target="tpu_custom_call" | custom-call | flops 7113539584 | bytes 27787264 | tf_op jit(solution)/shard_map/exchange/pallas_call | solution.py:351
  89.6 9.5 %finish.1 = f32[3584,512]{1,0:T(8,128)} custom-call(f32[3584,512]{1,0:T(8,128)} %get-tuple-element.8.summed, bf16[7,32,512]{2,1,0:T(8,128)(2,1)} %get-tuple-element.9.rotated, bf16[32,512]{1,0:T(8,128)(2,1)} %get-tuple-element.10.panel), custom_call_target="tpu_custom_call" | custom-call | flops 117440512 | bytes 14680064 | tf_op jit(solution)/shard_map/finish/pallas_call | solution.py:387

commit v3 on v2

--- a/solution.py
+++ b/solution.py
@@ -187,10 +187,6 @@
     if done < nc:
         lax.fori_loop(done, nc, lambda c, u: (rotate(c), u)[1], 0)
 
-    for direction in range(2):
-        in_copy(direction, half - 1, True).wait_recv()
-    own_small.wait()
-    panel_part[...] = jnp.dot(slab[...], basis_small[...], preferred_element_type=F32)
     share = panel_part.shape[0] // tn
 
     def share_rows(index):
@@ -208,9 +204,6 @@
         return pltpu.make_async_remote_copy(
             src_ref=ref, dst_ref=ref, send_sem=pg_send.at[k], recv_sem=pg_recv.at[k],
             device_id=(d, lax.rem(t + k, tn)), device_id_type=MESH)
-
-    for k in range(1, tn):
-        pr_copy(k).start()
 
     for s in range(1, half):
         def reduce_step(c, u, s=s):
@@ -234,6 +227,13 @@
             return u
         lax.fori_loop(0, nc, reduce_step, 0)
         if s == 1:
+            for direction in range(2):
+                in_copy(direction, half - 1, True).wait_recv()
+            own_small.wait()
+            panel_part[...] = jnp.dot(slab[...], basis_small[...], preferred_element_type=F32)
+            for k in range(1, tn):
+                pr_copy(k).start()
+        if s == 2:
             total = panel_part[share_rows(t)]
             for k in range(1, tn):
                 pr_copy(k).wait_recv()

time: 99.8 us -> 97.3 us (0.975)
  Pallas kernels: 98.5 us -> 96.3 us
    pallas_call x1, Pallas kernels: 89 us -> 86.8 us  [per_device(): pl.pallas_call(functools.partial(exchange_kernel, n, tn, nc, share_y), ou...]
where the time goes in v3:
time: 97.3 us; the launch traced here: 97 us
  Pallas kernels  96.3 us (99%)
    pallas_call x1, Pallas kernels, per_device(): pl.pallas_call(functools.partial(exchange_kernel, n, tn, nc, share_y), ou...  86.8 us
    pallas_call x1, Pallas kernels, per_device(): pl.pallas_call(functools.partial(finish_kernel, 1.0 / rows), out_shape=ja...  9.52 us

profile of v3, /device:TPU:0, one launch (start us, length us, event | category | flops | bytes accessed | tf_op | source)
XLA Modules:
  0.0 97.0 jit_solution(14288815917431824260)
XLA Ops:
  0.7 86.8 %exchange.1 = (f32[3584,512]{1,0:T(8,128)}, bf16[7,32,512]{2,1,0:T(8,128)(2,1)}, bf16[32,512]{1,0:T(8,128)(2,1)}) custom-call(bf16[32,28672]{1,0:T(8,128)(2,1)} %grads.1, bf16[32,8192]{1,0:T(8,128)(2,1)} %inputs.1, bf16[3584,3584]{1,0:T(8,128)(2,1)} %basis_out.1, bf16[2048,512]{1,0:T(8,128)(2,1)} %basis_in.1, s32[1]{0:T(128)S(6)} %copy.6.lengths), custom_call_target="tpu_custom_call" | custom-call | flops 7113539584 | bytes 27787264 | tf_op jit(solution)/shard_map/exchange/pallas_call | solution.py:351
  87.5 9.5 %finish.1 = f32[3584,512]{1,0:T(8,128)} custom-call(f32[3584,512]{1,0:T(8,128)} %get-tuple-element.8.summed, bf16[7,32,512]{2,1,0:T(8,128)(2,1)} %get-tuple-element.9.rotated, bf16[32,512]{1,0:T(8,128)(2,1)} %get-tuple-element.10.panel), custom_call_target="tpu_custom_call" | custom-call | flops 117440512 | bytes 14680064 | tf_op jit(solution)/shard_map/finish/pallas_call | solution.py:387
